TPU v7x, 32 devices: a whole 2x2x4 slice. The times are simulated.
32 devices in a mesh: row: 8 (over z, y), vec: 4 (over x, core).
Axes of the slice: x: 2, y: 2, z: 4, core: 2. Of those that a mesh axis runs over, the one named last changes fastest.
Arguments:
- vectors: float32 [8192, 6144], P('row', 'vec'), may hold values from -6 to 6
- reflectors: float32 [32, 512, 256], P('row', 'vec'), may hold values from -0.25 to 0.25
- inner_factors: float32 [32, 256, 256], P('row', 'vec'), may hold values from -0.375 to 0.375
- offsets: int32 [2, 16], P(None, 'row'), may hold values from 0 to 7680, as said below
- owners: int32 [2, 16], P(None, 'row'), may hold values from 0 to 3, as said below
Outputs:
- result: float32 [8192, 6144], P('row', 'vec')
Inputs may be any that keep to these rules, and one draw needn't show every extreme that they name: `offsets`: within each sweep the columns j * 2 to (j + 1) * 2 - 1 belong to panel j, the rows j * 1024 to (j + 1) * 1024 - 1; a panel's start rows increase and are multiples of 256. A first-sweep block lies within its panel. A second-sweep block starts 256 rows or more after its panel's first row; in every panel but the last, the last second-sweep block starts at the panel's end minus 256, so it runs 256 rows into the next panel; the last panel's second-sweep blocks lie within it. `owners`: for each panel, its 4 entries (both sweeps) are a permutation of 0 to 3.
All inputs are finite; a program needn't handle non-finite values.
Results may differ from a plain program's by a relative error of at most 0.0001.
Values sent between devices are 32-bit elements; how exact they have to be, the bound alone decides.
A program may use at most 64 MiB of HBM per device.

v0:
```python
import jax
import jax.numpy as jnp
from jax import lax
from jax.sharding import PartitionSpec as P


def from_behind(block, axis, distance):
    devices = range(lax.axis_size(axis))
    route = [(i - distance, i) for i in devices if i - distance in devices]
    return lax.ppermute(block, axis, route)


def contract_rows(left, right):
    return lax.dot_general(
        left,
        right,
        (((0,), (0,)), ((), ())),
        precision=lax.Precision.HIGHEST,
        preferred_element_type=jnp.float32,
    )


def multiply(left, right):
    return jnp.dot(left, right, precision=lax.Precision.HIGHEST, preferred_element_type=jnp.float32)


def shards(vectors, reflectors, inner_factors, offsets, owners):
    rows_dev = vectors.shape[0]
    reflect_count = reflectors.shape[2]
    block_rows = 2 * reflect_count
    per_sweep = offsets.shape[1]
    first_row = lax.axis_index("row") * rows_dev

    def fetch_block(owner_code):
        stored_basis = lax.dynamic_index_in_dim(reflectors, owner_code, 0, keepdims=False)
        stored_inner = lax.dynamic_index_in_dim(inner_factors, owner_code, 0, keepdims=False)
        return (
            lax.all_gather(stored_basis, "vec", axis=0, tiled=True),
            lax.all_gather(stored_inner, "vec", axis=0, tiled=True),
        )

    def run_sweep(current, sweep_index):

        def apply_block(block_index, current_rows):
            start_row = offsets[sweep_index, block_index] - first_row
            basis_block, inner_block = fetch_block(owners[sweep_index, block_index])
            window = lax.dynamic_slice_in_dim(current_rows, start_row, block_rows, 0)
            projection = contract_rows(basis_block, window)
            coupled = multiply(inner_block, projection)
            window = window - multiply(basis_block, coupled)
            return lax.dynamic_update_slice_in_dim(current_rows, window, start_row, 0)

        return lax.fori_loop(0, per_sweep, apply_block, current)

    after_first = run_sweep(vectors, 0)
    below_rows = from_behind(after_first[:reflect_count], "row", -1)
    extended = jnp.concatenate([after_first, below_rows], 0)
    extended = run_sweep(extended, 1)
    handed = from_behind(extended[rows_dev:], "row", 1)
    head_rows = jnp.where(lax.axis_index("row") > 0, handed, extended[:reflect_count])
    return jnp.concatenate([head_rows, extended[reflect_count:rows_dev]], 0)


def solution(mesh):
    return jax.shard_map(
        shards,
        mesh=mesh,
        in_specs=(
            P("row", "vec"),
            P("row", "vec", None),
            P("row", "vec", None),
            P(None, "row"),
            P(None, "row"),
        ),
        out_specs=P("row", "vec"),
        check_vma=False,
    )
```

profile of v0, /device:TPU:16, one launch (start us, length us, event | category | flops | bytes accessed | tf_op | source)
XLA Modules:
  0.0 240.6 jit_solution(6180024644845947862)
XLA Ops:
  0.0 6.0 %copy.21 = f32[1024,1536]{1,0:T(8,128)} copy(f32[1024,1536]{1,0:T(8,128)} %param.9) | data formatting | bytes 12582912
  6.0 69.2 %while.26 = (s32[]{:T(128)}, f32[1024,1536]{1,0:T(8,128)}, s32[2,2]{1,0:T(2,128)S(1)}, s32[]{:T(128)}, s32[2,2]{1,0:T(2,128)S(1)}, /*index=5*/f32[4,128,256]{2,1...) while((s32[]{:T(128)}, f32[1024,1536]{1,0:T(8,128)}, ...), condition=%wide.region_1.2_spmd, body=%wide.region_0.1_spmd.sunk | while | flops 6040584192 | bytes 49873164 | solution.py:53
  10.4 5.8 %all-gather.9 = f32[1,256,256]{2,1,0:T(8,128)S(1)} all-gather(f32[1,64,256]{2,1,0:T(8,128)S(1)} %constant_dynamic-slice_fusion.19), channel_id=3, replica_groups=mesh['row'=8,'vec'=4] {'vec'}, dimensions={1}, use_global_device_ids=true | all-gather | bytes 327680 | tf_op jit(solution)/shard_map/while/body/eval_jaxpr/all_gather | solution.py:39
  16.1 7.3 %all-gather.8 = f32[1,512,256]{2,1,0:T(8,128)S(1)} all-gather(f32[1,128,256]{2,1,0:T(8,128)S(1)} %constant_dynamic-slice_fusion.18), channel_id=2, replica_groups=mesh['row'=8,'vec'=4] {'vec'}, dimensions={1}, use_global_device_ids=true | all-gather | bytes 655360 | tf_op jit(solution)/shard_map/while/body/eval_jaxpr/all_gather | solution.py:38
  23.4 5.0 %fusion.40 = f32[256,1536]{1,0:T(8,128)S(1)} fusion(f32[1024,1536]{1,0:T(8,128)} %get-tuple-element.381, s32[]{:T(128)S(6)} %select_n.62, f32[1,512,256]{2,1,0:T(8,128)S(1)} %all-gather.8), kind=kOutput, calls=%fused_computation.1.clone.1 | convolution fusion | flops 2415919104 | bytes 5242884 | tf_op jit(solution)/shard_map/while/body/eval_jaxpr/dot_general | solution.py:14
  32.9 7.7 %dynamic_update_slice.16 = f32[1024,1536]{1,0:T(8,128)} dynamic-update-slice(f32[1024,1536]{1,0:T(8,128)} %get-tuple-element.381, f32[512,1536]{1,0:T(8,128)S(1)} %convolution_subtract_fusion.4, s32[]{:T(128)S(6)} %select_n.62, s32[]{:T(128)} %constant.86.clone.1..sunk) | dynamic-update-slice | bytes 6291460 | tf_op jit(solution)/shard_map/while/body/eval_jaxpr/dynamic_update_slice | solution.py:51
  44.9 5.9 %all-gather.9 = f32[1,256,256]{2,1,0:T(8,128)S(1)} all-gather(f32[1,64,256]{2,1,0:T(8,128)S(1)} %constant_dynamic-slice_fusion.19), channel_id=3, replica_groups=mesh['row'=8,'vec'=4] {'vec'}, dimensions={1}, use_global_device_ids=true | all-gather | bytes 327680 | tf_op jit(solution)/shard_map/while/body/eval_jaxpr/all_gather | solution.py:39
  50.8 7.3 %all-gather.8 = f32[1,512,256]{2,1,0:T(8,128)S(1)} all-gather(f32[1,128,256]{2,1,0:T(8,128)S(1)} %constant_dynamic-slice_fusion.18), channel_id=2, replica_groups=mesh['row'=8,'vec'=4] {'vec'}, dimensions={1}, use_global_device_ids=true | all-gather | bytes 655360 | tf_op jit(solution)/shard_map/while/body/eval_jaxpr/all_gather | solution.py:38
  58.1 4.9 %fusion.40 = f32[256,1536]{1,0:T(8,128)S(1)} fusion(f32[1024,1536]{1,0:T(8,128)} %get-tuple-element.381, s32[]{:T(128)S(6)} %select_n.62, f32[1,512,256]{2,1,0:T(8,128)S(1)} %all-gather.8), kind=kOutput, calls=%fused_computation.1.clone.1 | convolution fusion | flops 2415919104 | bytes 5242884 | tf_op jit(solution)/shard_map/while/body/eval_jaxpr/dot_general | solution.py:14
  67.5 7.6 %dynamic_update_slice.16 = f32[1024,1536]{1,0:T(8,128)} dynamic-update-slice(f32[1024,1536]{1,0:T(8,128)} %get-tuple-element.381, f32[512,1536]{1,0:T(8,128)S(1)} %convolution_subtract_fusion.4, s32[]{:T(128)S(6)} %select_n.62, s32[]{:T(128)} %constant.86.clone.1..sunk) | dynamic-update-slice | bytes 6291460 | tf_op jit(solution)/shard_map/while/body/eval_jaxpr/dynamic_update_slice | solution.py:51
  80.2 35.0 %collective-permute-done = f32[256,1536]{1,0:T(8,128)S(1)} collective-permute-done((f32[256,1536]{1,0:T(8,128)S(1)}, f32[256,1536]{1,0:T(8,128)S(1)}, u32[]{:S(2)}, u32[]{:S(2)}) %collective-permute-start) | collective-permute-done | bytes 1572896 | tf_op jit(solution)/shard_map/ppermute | solution.py:10
  115.2 6.5 %pad_maximum_fusion = f32[1280,1536]{1,0:T(8,128)} fusion(f32[256,1536]{1,0:T(8,128)S(1)} %collective-permute-done, f32[1024,1536]{1,0:T(8,128)} %get-tuple-element.253), kind=kLoop, calls=%fused_computation.24 | loop fusion | flops 1966080 | bytes 15728640 | tf_op jit(solution)/shard_map/concatenate | solution.py:57
  121.7 73.2 %while.27 = (s32[]{:T(128)}, f32[1280,1536]{1,0:T(8,128)}, s32[2,2]{1,0:T(2,128)S(1)}, s32[]{:T(128)}, s32[2,2]{1,0:T(2,128)S(1)}, /*index=5*/f32[4,128,256]{2,1...) while((s32[]{:T(128)}, f32[1280,1536]{1,0:T(8,128)}, ...), condition=%wide.region_3.4_spmd, body=%wide.region_2.3_spmd.sunk | while | flops 6040584192 | bytes 24707312 | solution.py:53
  126.4 5.8 %all-gather.11 = f32[1,256,256]{2,1,0:T(8,128)S(1)} all-gather(f32[1,64,256]{2,1,0:T(8,128)S(1)} %constant_dynamic-slice_fusion.23), channel_id=5, replica_groups=mesh['row'=8,'vec'=4] {'vec'}, dimensions={1}, use_global_device_ids=true | all-gather | bytes 327680 | tf_op jit(solution)/shard_map/while/body/eval_jaxpr/all_gather | solution.py:39
  132.2 7.3 %all-gather.10 = f32[1,512,256]{2,1,0:T(8,128)S(1)} all-gather(f32[1,128,256]{2,1,0:T(8,128)S(1)} %constant_dynamic-slice_fusion.22), channel_id=4, replica_groups=mesh['row'=8,'vec'=4] {'vec'}, dimensions={1}, use_global_device_ids=true | all-gather | bytes 655360 | tf_op jit(solution)/shard_map/while/body/eval_jaxpr/all_gather | solution.py:38
  139.5 4.8 %fusion.48 = f32[256,1536]{1,0:T(8,128)S(1)} fusion(f32[1280,1536]{1,0:T(8,128)} %get-tuple-element.414, s32[]{:T(128)S(6)} %select_n.64, f32[1,512,256]{2,1,0:T(8,128)S(1)} %all-gather.10), kind=kOutput, calls=%fused_computation.13.clone.1 | convolution fusion | flops 2415919104 | bytes 5242884 | tf_op jit(solution)/shard_map/while/body/eval_jaxpr/dot_general | solution.py:14
  145.8 4.8 %convolution_subtract_fusion.5 = f32[512,1536]{1,0:T(8,128)S(1)} fusion(f32[256,1536]{1,0:T(8,128)S(1)} %fusion.49, f32[1280,1536]{1,0:T(8,128)} %get-tuple-element.414, s32[]{:T(128)S(6)} %select_n.64, f32[1,512,256]{2,1,0:T(8,128)S(1)} %all-gather.10), kind=kOutput, calls=%fused_computation.12.clone.1 | convolution fusion | flops 2416705536 | bytes 8388612 | tf_op jit(solution)/shard_map/while/body/eval_jaxpr/dot_general | solution.py:24
  150.6 7.7 %dynamic_update_slice.17 = f32[1280,1536]{1,0:T(8,128)} dynamic-update-slice(f32[1280,1536]{1,0:T(8,128)} %get-tuple-element.414, f32[512,1536]{1,0:T(8,128)S(1)} %convolution_subtract_fusion.5, s32[]{:T(128)S(6)} %select_n.64, s32[]{:T(128)} %constant.86.clone.1..sunk.1) | dynamic-update-slice | bytes 6291460 | tf_op jit(solution)/shard_map/while/body/eval_jaxpr/dynamic_update_slice | solution.py:51
  163.0 5.9 %all-gather.11 = f32[1,256,256]{2,1,0:T(8,128)S(1)} all-gather(f32[1,64,256]{2,1,0:T(8,128)S(1)} %constant_dynamic-slice_fusion.23), channel_id=5, replica_groups=mesh['row'=8,'vec'=4] {'vec'}, dimensions={1}, use_global_device_ids=true | all-gather | bytes 327680 | tf_op jit(solution)/shard_map/while/body/eval_jaxpr/all_gather | solution.py:39
  168.9 7.3 %all-gather.10 = f32[1,512,256]{2,1,0:T(8,128)S(1)} all-gather(f32[1,128,256]{2,1,0:T(8,128)S(1)} %constant_dynamic-slice_fusion.22), channel_id=4, replica_groups=mesh['row'=8,'vec'=4] {'vec'}, dimensions={1}, use_global_device_ids=true | all-gather | bytes 655360 | tf_op jit(solution)/shard_map/while/body/eval_jaxpr/all_gather | solution.py:38
  176.2 4.8 %fusion.48 = f32[256,1536]{1,0:T(8,128)S(1)} fusion(f32[1280,1536]{1,0:T(8,128)} %get-tuple-element.414, s32[]{:T(128)S(6)} %select_n.64, f32[1,512,256]{2,1,0:T(8,128)S(1)} %all-gather.10), kind=kOutput, calls=%fused_computation.13.clone.1 | convolution fusion | flops 2415919104 | bytes 5242884 | tf_op jit(solution)/shard_map/while/body/eval_jaxpr/dot_general | solution.py:14
  182.4 4.8 %convolution_subtract_fusion.5 = f32[512,1536]{1,0:T(8,128)S(1)} fusion(f32[256,1536]{1,0:T(8,128)S(1)} %fusion.49, f32[1280,1536]{1,0:T(8,128)} %get-tuple-element.414, s32[]{:T(128)S(6)} %select_n.64, f32[1,512,256]{2,1,0:T(8,128)S(1)} %all-gather.10), kind=kOutput, calls=%fused_computation.12.clone.1 | convolution fusion | flops 2416705536 | bytes 8388612 | tf_op jit(solution)/shard_map/while/body/eval_jaxpr/dot_general | solution.py:24
  187.2 7.6 %dynamic_update_slice.17 = f32[1280,1536]{1,0:T(8,128)} dynamic-update-slice(f32[1280,1536]{1,0:T(8,128)} %get-tuple-element.414, f32[512,1536]{1,0:T(8,128)S(1)} %convolution_subtract_fusion.5, s32[]{:T(128)S(6)} %select_n.64, s32[]{:T(128)} %constant.86.clone.1..sunk.1) | dynamic-update-slice | bytes 6291460 | tf_op jit(solution)/shard_map/while/body/eval_jaxpr/dynamic_update_slice | solution.py:51
  203.4 32.4 %collective-permute-done.1 = f32[256,1536]{1,0:T(8,128)S(1)} collective-permute-done((f32[256,1536]{1,0:T(8,128)S(1)}, f32[256,1536]{1,0:T(8,128)S(1)}, u32[]{:S(2)}, u32[]{:S(2)}) %collective-permute-start.1) | collective-permute-done | bytes 1572896 | tf_op jit(solution)/shard_map/ppermute | solution.py:10
  (39 shorter events, 38.5 us)
Async XLA Ops:
  0.0 6.0 %copy-start.1 = (f32[4,64,256]{2,1,0:T(8,128)S(1)}, f32[4,64,256]{2,1,0:T(8,128)}, u32[]{:S(2)}) copy-start(f32[4,64,256]{2,1,0:T(8,128)} %param.11) | copy-start | bytes 786436
  0.0 6.0 %copy-start.2 = (s32[2,2]{1,0:T(2,128)S(1)}, s32[2,2]{1,0:T(2,128)}, u32[]{:S(2)}) copy-start(s32[2,2]{1,0:T(2,128)} %param.12) | copy-start | bytes 52
  0.0 6.0 %copy-start.3 = (s32[2,2]{1,0:T(2,128)S(1)}, s32[2,2]{1,0:T(2,128)}, u32[]{:S(2)}) copy-start(s32[2,2]{1,0:T(2,128)} %param.13) | copy-start | bytes 52
  23.4 6.4 %copy-start = (f32[1024,1536]{1,0:T(8,128)S(1)}, f32[1024,1536]{1,0:T(8,128)}, u32[]{:S(2)}) copy-start(f32[1024,1536]{1,0:T(8,128)} %get-tuple-element.381) | copy-start | bytes 18874372 | tf_op jit(solution)/shard_map/while
  58.1 6.4 %copy-start = (f32[1024,1536]{1,0:T(8,128)S(1)}, f32[1024,1536]{1,0:T(8,128)}, u32[]{:S(2)}) copy-start(f32[1024,1536]{1,0:T(8,128)} %get-tuple-element.381) | copy-start | bytes 18874372 | tf_op jit(solution)/shard_map/while
  76.7 38.5 %collective-permute-start = (f32[256,1536]{1,0:T(8,128)S(1)}, f32[256,1536]{1,0:T(8,128)S(1)}, u32[]{:S(2)}, u32[]{:S(2)}) collective-permute-start(f32[256,1536]{1,0:T(8,128)S(1)} %slice.12), channel_id=1, source_target_pairs={{4,0},{8,4},{12,8},{16,12},{20,16},{24,20},{28,24},{5,1},{9,5},{13... | collective-permute-start | bytes 4718600 | tf_op jit(solution)/shard_map/ppermute | solution.py:10
  196.4 39.4 %collective-permute-start.1 = (f32[256,1536]{1,0:T(8,128)S(1)}, f32[256,1536]{1,0:T(8,128)S(1)}, u32[]{:S(2)}, u32[]{:S(2)}) collective-permute-start(f32[256,1536]{1,0:T(8,128)S(1)} %slice.13), channel_id=1, source_target_pairs={{0,4},{4,8},{8,12},{12,16},{16,20},{20,24},{24,28},{1,5},{5,9},{9,... | collective-permute-start | bytes 4718600 | tf_op jit(solution)/shard_map/ppermute | solution.py:10
where the time goes:
time: 243 us; the launch traced here: 241 us
  waiting for transfers between devices  67.5 us (28%)
  blocking collectives  52.4 us (22%)
  local copies, waits for them, and re-layouts  50.8 us (21%)
  matrix products  41 us (17%)
  other arithmetic  11.2 us (5%)
  loops' own time  9.88 us (4%)
  starting transfers between devices  7.82 us (3%)
    ppermute x2, waiting for transfers between devices, from_behind(): return lax.ppermute(block, axis, route)  67.5 us
    dynamic_update_slice x4, local copies, waits for them, and re-layouts, apply_block(): return lax.dynamic_update_slice_in_dim(current_rows, window, start_row, 0)  30.7 us
    all_gather x4, blocking collectives, fetch_block(): lax.all_gather(stored_basis, 'vec', axis=0, tiled=True)  29.1 us
    all_gather x4, blocking collectives, fetch_block(): lax.all_gather(stored_inner, 'vec', axis=0, tiled=True)  23.3 us
    dot_general x8, matrix products, multiply(): jnp.dot(left, right, precision=lax.Precision.HIGHEST, preferred_element_t...  21.5 us
    dot_general x4, matrix products, contract_rows(): lax.dot_general(left, right, (((0,), (0,)), ((), ())), precision=lax.Prec...  19.5 us
    another operation x2, loops' own time, run_sweep(): return lax.fori_loop(0, per_sweep, apply_block, current)  9.88 us
    ppermute x2, starting transfers between devices, from_behind(): return lax.ppermute(block, axis, route)  7.82 us
  transfers between devices with their start and end apart: 2, of which 2 were waited for; matrix products, arithmetic and copies ran while one was open for 1% of the time, Pallas kernels for 0%

commit v1 on v0

v1 whole, which is shorter than its diff:
```python
import functools

import jax
import jax.numpy as jnp
from jax import lax
from jax.experimental import pallas as pl
from jax.experimental.pallas import tpu as pltpu
from jax.sharding import PartitionSpec as P

MESH = pl.DeviceIdType.MESH


def split(value):
    high = value.astype(jnp.bfloat16)
    low = (value - high.astype(jnp.float32)).astype(jnp.bfloat16)
    return high, low


def dot(left, right):
    return jnp.dot(left, right, preferred_element_type=jnp.float32)


def dot_split(left_high, left_low, right):
    right_high, right_low = split(right)
    return dot(left_high, right_high) + (dot(left_high, right_low) + dot(left_low, right_high))


def kernel(
    panels, members, per_sweep, step, chunks, width,
    places, owners, vectors, reflectors, inner, out,
    current, below, update, gathered, basis_high, basis_low, mixed_high, mixed_low,
    load_sem, store_sem, head_sem, part_send, part_recv, back_send, back_recv, fore_send, fore_recv,
):
    panel = lax.axis_index("row")
    me = lax.axis_index("vec")
    core = lax.rem(me, 2)
    chip = me // 2
    chips = members // 2
    sibling = chip * 2 + 1 - core
    units = vectors.shape[0]
    basis_rows = reflectors.shape[1]
    is_first = panel == 0
    is_last = panel == panels - 1
    stored = [(sweep, index) for sweep in range(2) for index in range(per_sweep)]

    def columns(chunk):
        return pl.ds(pl.multiple_of(chunk * width, width), width)

    def load(chunk):
        return pltpu.make_async_copy(vectors.at[:, :, columns(chunk)], current.at[chunk], load_sem.at[chunk])

    def store(chunk):
        return pltpu.make_async_copy(
            current.at[chunk, pl.ds(1, units - 1)],
            out.at[pl.ds(1, units - 1), :, columns(chunk)],
            store_sem.at[chunk],
        )

    def store_head(chunk):
        return pltpu.make_async_copy(
            current.at[chunk, 0], out.at[0, :, columns(chunk)], head_sem.at[chunk]
        )

    def send_back(chunk):
        return pltpu.make_async_remote_copy(
            src_ref=current.at[chunk, 0],
            dst_ref=below.at[chunk],
            send_sem=back_send.at[chunk],
            recv_sem=back_recv.at[chunk],
            device_id=(panel - 1, me),
            device_id_type=MESH,
        )

    def send_fore(chunk):
        return pltpu.make_async_remote_copy(
            src_ref=below.at[chunk],
            dst_ref=out.at[0, :, columns(chunk)],
            send_sem=fore_send.at[chunk],
            recv_sem=fore_recv.at[chunk],
            device_id=(panel + 1, me),
            device_id_type=MESH,
        )

    def send_part(block, part, slot, target):
        return pltpu.make_async_remote_copy(
            src_ref=gathered.at[block, part],
            dst_ref=gathered.at[block, part],
            send_sem=part_send.at[block, slot],
            recv_sem=part_recv.at[block, part],
            device_id=(panel, target),
            device_id_type=MESH,
        )

    def other_chip(distance):
        return lax.rem(chip + distance, chips)

    def each(body):
        lax.fori_loop(0, chunks, lambda chunk, _: (body(chunk), 0)[1], 0)

    each(lambda chunk: load(chunk).start())

    barrier = pltpu.get_barrier_semaphore()

    def greet(row, vec):
        pl.semaphore_signal(barrier, inc=1, device_id=(row, vec), device_id_type=MESH)

    greet(panel, sibling)
    for distance in range(1, chips):
        greet(panel, other_chip(distance) * 2 + core)

    @pl.when(jnp.logical_not(is_first))
    def _():
        greet(panel - 1, me)

    @pl.when(jnp.logical_not(is_last))
    def _():
        greet(panel + 1, me)

    for block, (sweep, index) in enumerate(stored):
        owner = owners[sweep, index]
        gathered[block, me, :basis_rows, :] = reflectors[owner]
        gathered[block, me, basis_rows:, :] = inner[owner]

    update[0] = jnp.zeros_like(update[0])
    update[3] = jnp.zeros_like(update[3])

    pl.semaphore_wait(barrier, chips + jnp.minimum(panel, 1) + jnp.minimum(panels - 1 - panel, 1))

    for block in range(len(stored)):
        for distance in range(1, chips):
            send_part(block, me, distance, other_chip(distance) * 2 + core).start()
        send_part(block, me, 0, sibling).start()

    def fetch(block):
        for distance in range(1, chips):
            part = other_chip(distance) * 2 + core
            send_part(block, part, distance, part).wait_recv()
            send_part(block, part, chips - 1 + distance, sibling).start()
        send_part(block, sibling, 0, sibling).wait_recv()
        for distance in range(1, chips):
            part = other_chip(distance) * 2 + 1 - core
            send_part(block, part, chips - 1 + distance, sibling).wait_recv()
        basis = gathered[block, :, :basis_rows, :].reshape(2 * step, step)
        coupling = gathered[block, :, basis_rows:, :].reshape(step, step)
        high, low = split(basis)
        mixed_high[block], mixed_low[block] = split(dot_split(high, low, coupling))
        basis_high[block], basis_low[block] = split(basis.T)

    def change(block, upper, lower):
        window = jnp.concatenate([upper, lower], 0)
        projection = dot_split(basis_high[block], basis_low[block], window)
        moved = dot_split(mixed_high[block], mixed_low[block], projection)
        update[1] = moved[:step]
        update[2] = moved[step:]

    def apply_change(block, chunk, lowest):
        for unit in range(lowest, units):
            current[chunk, unit] = current[chunk, unit] - update[places[block, 2 + unit]]

    each(lambda chunk: load(chunk).wait())

    for block, (sweep, index) in enumerate(stored[:-1]):
        fetch(block)

        def run(chunk, block=block, lowest=sweep + index):
            change(block, current[chunk, places[block, 0]], current[chunk, places[block, 1]])
            apply_change(block, chunk, lowest)
            if block == 0:

                @pl.when(jnp.logical_not(is_first))
                def _():
                    send_back(chunk).start()

                @pl.when(is_first)
                def _():
                    store_head(chunk).start()

        each(run)

    last = len(stored) - 1
    fetch(last)

    def finish(chunk):
        @pl.when(is_last)
        def _():
            below[chunk] = current[chunk, places[last, 1]]

        @pl.when(jnp.logical_not(is_last))
        def _():
            send_back(chunk).wait_recv()

        change(last, current[chunk, places[last, 0]], below[chunk])

        @pl.when(jnp.logical_not(is_last))
        def _():
            below[chunk] = below[chunk] - update[2]
            send_fore(chunk).start()

        apply_change(last, chunk, per_sweep)
        store(chunk).start()

    each(finish)

    for block in range(len(stored)):
        for slot in range(members - 1):
            send_part(block, me, slot, sibling).wait_send()

    @pl.when(is_first)
    def _():
        each(lambda chunk: store_head(chunk).wait())

    @pl.when(jnp.logical_not(is_first))
    def _():
        each(lambda chunk: send_back(chunk).wait_send())

    each(lambda chunk: store(chunk).wait())

    @pl.when(jnp.logical_not(is_last))
    def _():
        each(lambda chunk: send_fore(chunk).wait_send())

    @pl.when(jnp.logical_not(is_first))
    def _():
        each(lambda chunk: send_fore(chunk).wait_recv())


def shards(panels, members, vectors, reflectors, inner_factors, offsets, owners):
    rows_dev, cols = vectors.shape
    blocks, basis_rows, step = reflectors.shape
    inner_rows = inner_factors.shape[1]
    per_sweep = offsets.shape[1]
    width = 256 if cols % 256 == 0 else 128
    chunks = cols // width
    units = rows_dev // step
    first_unit = (offsets - lax.axis_index("row") * rows_dev).reshape(-1, 1) // step
    unit_at = jnp.arange(units, dtype=jnp.int32)
    places = jnp.concatenate(
        [first_unit, jnp.minimum(first_unit + 1, units - 1), jnp.clip(unit_at - first_unit + 1, 0, 3)], 1
    )
    smem = pl.BlockSpec(memory_space=pltpu.SMEM)
    vmem = pl.BlockSpec(memory_space=pltpu.VMEM)
    anywhere = pl.BlockSpec(memory_space=pl.ANY)
    dma = pltpu.SemaphoreType.DMA
    result = pl.pallas_call(
        functools.partial(kernel, panels, members, per_sweep, step, chunks, width),
        out_shape=jax.ShapeDtypeStruct((units, step, cols), jnp.float32),
        in_specs=[smem, smem, anywhere, vmem, vmem],
        out_specs=anywhere,
        scratch_shapes=[
            pltpu.VMEM((chunks, units, step, width), jnp.float32),
            pltpu.VMEM((chunks, step, width), jnp.float32),
            pltpu.VMEM((4, step, width), jnp.float32),
            pltpu.VMEM((blocks, members, basis_rows + inner_rows, step), jnp.float32),
            pltpu.VMEM((blocks, step, 2 * step), jnp.bfloat16),
            pltpu.VMEM((blocks, step, 2 * step), jnp.bfloat16),
            pltpu.VMEM((blocks, 2 * step, step), jnp.bfloat16),
            pltpu.VMEM((blocks, 2 * step, step), jnp.bfloat16),
            dma((chunks,)),
            dma((chunks,)),
            dma((chunks,)),
            dma((blocks, members - 1)),
            dma((blocks, members)),
            dma((chunks,)),
            dma((chunks,)),
            dma((chunks,)),
            dma((chunks,)),
        ],
        compiler_params=pltpu.CompilerParams(
            collective_id=0, has_side_effects=True, vmem_limit_bytes=48 * 1024 * 1024
        ),
        cost_estimate=pl.CostEstimate(
            flops=2 * 3 * 4 * blocks * step * step * cols,
            bytes_accessed=2 * 4 * rows_dev * cols,
            transcendentals=0,
        ),
    )(places, owners, vectors.reshape(units, step, cols), reflectors, inner_factors)
    return result.reshape(rows_dev, cols)


def solution(mesh):
    return jax.shard_map(
        functools.partial(shards, mesh.shape["row"], mesh.shape["vec"]),
        mesh=mesh,
        in_specs=(
            P("row", "vec"),
            P("row", "vec", None),
            P("row", "vec", None),
            P(None, "row"),
            P(None, "row"),
        ),
        out_specs=P("row", "vec"),
        check_vma=False,
    )
```

time: 243 us -> 100 us (0.41)
  Pallas kernels: 0 us -> 89.2 us
  waiting for transfers between devices: 67.5 us -> 0 us
  blocking collectives: 52.4 us -> 0 us
  local copies, waits for them, and re-layouts: 50.8 us -> 8.77 us
  matrix products: 41 us -> 0 us
  other arithmetic: 11.2 us -> 0.85 us
  loops' own time: 9.88 us -> 0 us
  starting transfers between devices: 7.82 us -> 0 us
    pallas_call x0 -> x1, Pallas kernels: none -> 89.2 us  [shards(): pl.pallas_call(functools.partial(kernel, panels, members, per_sweep, step...]
    ppermute x2 -> x0, waiting for transfers between devices: 67.5 us -> none  [from_behind(): return lax.ppermute(block, axis, route)]
    all_gather x8 -> x0, blocking collectives: 52.4 us -> none  [the longest x4 29.1 us: fetch_block(): lax.all_gather(stored_basis, 'vec', axis=0, tiled=True)]
    dot_general x12 -> x0, matrix products: 41 us -> none  [the longest x8 21.5 us: multiply(): jnp.dot(left, right, precision=lax.Precision.HIGHEST, preferred_element_t...]
    dynamic_update_slice x4 -> x0, local copies, waits for them, and re-layouts: 30.7 us -> none  [apply_block(): return lax.dynamic_update_slice_in_dim(current_rows, window, start_row, 0)]
    another operation x2 -> x0, loops' own time: 9.88 us -> none  [run_sweep(): return lax.fori_loop(0, per_sweep, apply_block, current)]
    concatenate x2 -> x1, other arithmetic: 9.64 us -> 0.08 us  [shards(): jnp.concatenate([first_unit, jnp.minimum(first_unit + 1, units - 1), jnp....]
    dynamic_slice x16 -> x0, local copies, waits for them, and re-layouts: 8.38 us -> none  [the longest x4 3.68 us: fetch_block(): lax.dynamic_index_in_dim(reflectors, owner_code, 0, keepdims=False)]
  transfers between devices with their start and end apart: 2 -> 0, of which waited for: 2 -> 0; matrix products, arithmetic and copies ran while one was open for 1% -> 0% of each run, Pallas kernels for 0% -> 0%
where the time goes in v1:
time: 100 us; the launch traced here: 98.8 us
  Pallas kernels  89.2 us (89%)
  local copies, waits for them, and re-layouts  8.77 us (9%)
    pallas_call x1, Pallas kernels, shards(): pl.pallas_call(functools.partial(kernel, panels, members, per_sweep, step...  89.2 us
    unnamed x7, local copies, waits for them, and re-layouts  8.6 us

profile of v1, /device:TPU:16, one launch (start us, length us, event | category | flops | bytes accessed | tf_op | source)
XLA Modules:
  0.0 98.8 jit_solution(12212286537186700752)
XLA Ops:
  0.0 0.7 broadcast_subtract_fusion
  0.7 0.1 reshape.144
  0.8 0.1 reshape.147
  0.9 0.1 add_clamp_fusion
  0.9 0.1 pad_add_fusion.places
  1.0 0.0 copy-start
  1.0 1.0 %copy-done = f32[4,128,256]{2,1,0:T(8,128)S(1)} copy-done((f32[4,128,256]{2,1,0:T(8,128)S(1)}, f32[4,128,256]{2,1,0:T(8,128)}, u32[]{:S(2)}) %copy-start) | copy-done | bytes 524312
  2.1 0.0 copy-start.1
  2.1 0.9 copy-done.1
  3.0 0.0 copy-start.2
  3.0 0.7 copy-done.2
  3.7 89.2 %shard_map.55 = f32[4,256,1536]{2,1,0:T(8,128)} custom-call(s32[4,6]{1,0:T(4,128)S(1)} %pad_add_fusion.places, s32[2,2]{1,0:T(2,128)S(1)} %copy-done.2, f32[4,256,1536]{2,1,0:T(8,128)} %bitcast.3, f32[4,128,256]{2,1,0:T(8,128)S(1)} %copy-done, f32[4,64,256]{2,1,0:T(8,128)S(1)} %copy-done.1), custom_call_target="tpu_custom_call" | custom-call | flops 9663676416 | bytes 12582912 | tf_op jit(solution)/shard_map/pallas_call | solution.py:244
  92.9 5.9 %copy.11 = f32[1024,1536]{1,0:T(8,128)} copy(f32[1024,1536]{1,0:T(8,128)} %bitcast.2) | data formatting | bytes 12582912
  (2 shorter events, 0.0 us)
Async XLA Ops:
  1.0 1.0 %copy-start = (f32[4,128,256]{2,1,0:T(8,128)S(1)}, f32[4,128,256]{2,1,0:T(8,128)}, u32[]{:S(2)}) copy-start(f32[4,128,256]{2,1,0:T(8,128)} %reflectors.1) | copy-start | bytes 1572868
  2.1 0.9 copy-start.1
  3.0 0.7 copy-start.2

commit v2 on v1

--- a/solution.py
+++ b/solution.py
@@ -27,9 +27,9 @@
 
 def kernel(
     panels, members, per_sweep, step, chunks, width,
-    places, owners, vectors, reflectors, inner, out,
-    current, below, update, gathered, basis_high, basis_low, mixed_high, mixed_low,
-    load_sem, store_sem, head_sem, part_send, part_recv, back_send, back_recv, fore_send, fore_recv,
+    offsets_in, owners_in, vectors, reflectors_in, inner_in, out,
+    offsets, owners, reflectors, inner, relay, current, below, update, gathered, basis_high, basis_low, mixed_high, mixed_low,
+    early_sem, relay_send, relay_recv, load_sem, store_sem, head_sem, part_send, part_recv, back_send, back_recv, fore_send, fore_recv,
 ):
     panel = lax.axis_index("row")
     me = lax.axis_index("vec")
@@ -39,6 +39,10 @@
     sibling = chip * 2 + 1 - core
     units = vectors.shape[0]
     basis_rows = reflectors.shape[1]
+    first_row = panel * units * step
+    pairs = panels // 2
+    is_odd = panel % 2 == 1
+    pair = panel // 2
     is_first = panel == 0
     is_last = panel == panels - 1
     stored = [(sweep, index) for sweep in range(2) for index in range(per_sweep)]
@@ -61,25 +65,94 @@
             current.at[chunk, 0], out.at[0, :, columns(chunk)], head_sem.at[chunk]
         )
 
+    def turn(chunk, share):
+        return ((chunk + 1) * share) // pairs - (chunk * share) // pairs == 1
+
+    def back_turn(chunk, source_pair):
+        return turn(chunk, pairs - source_pair)
+
+    def fore_turn(chunk, source_pair):
+        return turn(chunk, source_pair + 1)
+
+    def remote(source, target, send_sem, recv_sem, row):
+        return pltpu.make_async_remote_copy(
+            src_ref=source,
+            dst_ref=target,
+            send_sem=send_sem,
+            recv_sem=recv_sem,
+            device_id=(row, me),
+            device_id_type=MESH,
+        )
+
+    def head(chunk):
+        return out.at[0, :, columns(chunk)]
+
     def send_back(chunk):
-        return pltpu.make_async_remote_copy(
-            src_ref=current.at[chunk, 0],
-            dst_ref=below.at[chunk],
-            send_sem=back_send.at[chunk],
-            recv_sem=back_recv.at[chunk],
-            device_id=(panel - 1, me),
-            device_id_type=MESH,
-        )
+        return remote(current.at[chunk, 0], below.at[chunk], back_send.at[chunk], back_recv.at[chunk], panel - 1)
+
+    def send_back_far(chunk):
+        return remote(current.at[chunk, 0], relay.at[chunk], back_send.at[chunk], relay_recv.at[chunk], panel - 2)
 
     def send_fore(chunk):
-        return pltpu.make_async_remote_copy(
-            src_ref=below.at[chunk],
-            dst_ref=out.at[0, :, columns(chunk)],
-            send_sem=fore_send.at[chunk],
-            recv_sem=fore_recv.at[chunk],
-            device_id=(panel + 1, me),
-            device_id_type=MESH,
-        )
+        return remote(below.at[chunk], head(chunk), fore_send.at[chunk], fore_recv.at[chunk], panel + 1)
+
+    def send_fore_far(chunk):
+        return remote(below.at[chunk], relay.at[chunk], fore_send.at[chunk], relay_recv.at[chunk], panel + 2)
+
+    def pass_back(chunk):
+        return remote(relay.at[chunk], below.at[chunk], relay_send.at[chunk], back_recv.at[chunk], panel + 1)
+
+    def pass_fore(chunk):
+        return remote(relay.at[chunk], head(chunk), relay_send.at[chunk], fore_recv.at[chunk], panel - 1)
+
+    passes_back = jnp.logical_and(jnp.logical_not(is_odd), panel + 2 < panels)
+    passes_fore = jnp.logical_and(is_odd, panel > 1)
+
+    def both(left, right):
+        return jnp.logical_and(left, right)
+
+    def start_back(chunk):
+        far = both(jnp.logical_not(is_odd), back_turn(chunk, pair))
+
+        @pl.when(far)
+        def _():
+            send_back_far(chunk).start()
+
+        @pl.when(jnp.logical_not(far))
+        def _():
+            send_back(chunk).start()
+
+    def start_fore(chunk):
+        far = both(both(is_odd, panel + 2 < panels), fore_turn(chunk, pair))
+
+        @pl.when(far)
+        def _():
+            send_fore_far(chunk).start()
+
+        @pl.when(jnp.logical_not(far))
+        def _():
+            send_fore(chunk).start()
+
+    def hand_back(chunk):
+        @pl.when(both(passes_back, both(chunk < chunks, back_turn(chunk, pair + 1))))
+        def _():
+            send_back_far(chunk).wait_recv()
+            pass_back(chunk).start()
+
+    def hand_fore(chunk):
+        @pl.when(both(passes_fore, both(chunk >= 0, fore_turn(chunk, pair - 1))))
+        def _():
+            send_fore_far(chunk).wait_recv()
+            pass_fore(chunk).start()
+
+    def settle(chunk):
+        handed = jnp.logical_or(
+            both(passes_back, back_turn(chunk, pair + 1)), both(passes_fore, fore_turn(chunk, pair - 1))
+        )
+
+        @pl.when(handed)
+        def _():
+            pass_back(chunk).wait_send()
 
     def send_part(block, part, slot, target):
         return pltpu.make_async_remote_copy(
@@ -97,6 +170,14 @@
     def each(body):
         lax.fori_loop(0, chunks, lambda chunk, _: (body(chunk), 0)[1], 0)
 
+    early = [
+        pltpu.make_async_copy(source, target, early_sem.at[at])
+        for at, (source, target) in enumerate(
+            [(owners_in, owners), (offsets_in, offsets), (reflectors_in, reflectors), (inner_in, inner)]
+        )
+    ]
+    for copy in early:
+        copy.start()
     each(lambda chunk: load(chunk).start())
 
     barrier = pltpu.get_barrier_semaphore()
@@ -115,6 +196,17 @@
     @pl.when(jnp.logical_not(is_last))
     def _():
         greet(panel + 1, me)
+
+    @pl.when(panel > 1)
+    def _():
+        greet(panel - 2, me)
+
+    @pl.when(panel + 2 < panels)
+    def _():
+        greet(panel + 2, me)
+
+    for copy in early:
+        copy.wait()
 
     for block, (sweep, index) in enumerate(stored):
         owner = owners[sweep, index]
@@ -124,7 +216,9 @@
     update[0] = jnp.zeros_like(update[0])
     update[3] = jnp.zeros_like(update[3])
 
-    pl.semaphore_wait(barrier, chips + jnp.minimum(panel, 1) + jnp.minimum(panels - 1 - panel, 1))
+    beside = jnp.minimum(panel, 1) + jnp.minimum(panels - 1 - panel, 1)
+    beyond = jnp.minimum(panel // 2, 1) + jnp.minimum((panels - 1 - panel) // 2, 1)
+    pl.semaphore_wait(barrier, chips + beside + beyond)
 
     for block in range(len(stored)):
         for distance in range(1, chips):
@@ -153,9 +247,17 @@
         update[1] = moved[:step]
         update[2] = moved[step:]
 
+    def first_unit(block):
+        return jnp.maximum(offsets[stored[block][0], stored[block][1]] - first_row, 0) // step
+
+    def lower_unit(block):
+        return jnp.minimum(first_unit(block) + 1, units - 1)
+
     def apply_change(block, chunk, lowest):
+        first = first_unit(block)
         for unit in range(lowest, units):
-            current[chunk, unit] = current[chunk, unit] - update[places[block, 2 + unit]]
+            place = jnp.minimum(jnp.maximum(unit + 1 - first, 0), 3)
+            current[chunk, unit] = current[chunk, unit] - update[place]
 
     each(lambda chunk: load(chunk).wait())
 
@@ -163,13 +265,13 @@
         fetch(block)
 
         def run(chunk, block=block, lowest=sweep + index):
-            change(block, current[chunk, places[block, 0]], current[chunk, places[block, 1]])
+            change(block, current[chunk, first_unit(block)], current[chunk, lower_unit(block)])
             apply_change(block, chunk, lowest)
             if block == 0:
 
                 @pl.when(jnp.logical_not(is_first))
                 def _():
-                    send_back(chunk).start()
+                    start_back(chunk)
 
                 @pl.when(is_first)
                 def _():
@@ -183,23 +285,28 @@
     def finish(chunk):
         @pl.when(is_last)
         def _():
-            below[chunk] = current[chunk, places[last, 1]]
+            below[chunk] = current[chunk, lower_unit(last)]
 
         @pl.when(jnp.logical_not(is_last))
         def _():
             send_back(chunk).wait_recv()
 
-        change(last, current[chunk, places[last, 0]], below[chunk])
+        change(last, current[chunk, first_unit(last)], below[chunk])
 
         @pl.when(jnp.logical_not(is_last))
         def _():
             below[chunk] = below[chunk] - update[2]
-            send_fore(chunk).start()
-
+            start_fore(chunk)
+
+        hand_back(chunk + 1)
+        hand_fore(chunk - 1)
         apply_change(last, chunk, per_sweep)
         store(chunk).start()
 
+    hand_back(0)
     each(finish)
+    hand_fore(chunks - 1)
+    each(settle)
 
     for block in range(len(stored)):
         for slot in range(members - 1):
@@ -229,24 +336,22 @@
     blocks, basis_rows, step = reflectors.shape
     inner_rows = inner_factors.shape[1]
     per_sweep = offsets.shape[1]
-    width = 256 if cols % 256 == 0 else 128
+    width = 128
     chunks = cols // width
     units = rows_dev // step
-    first_unit = (offsets - lax.axis_index("row") * rows_dev).reshape(-1, 1) // step
-    unit_at = jnp.arange(units, dtype=jnp.int32)
-    places = jnp.concatenate(
-        [first_unit, jnp.minimum(first_unit + 1, units - 1), jnp.clip(unit_at - first_unit + 1, 0, 3)], 1
-    )
-    smem = pl.BlockSpec(memory_space=pltpu.SMEM)
-    vmem = pl.BlockSpec(memory_space=pltpu.VMEM)
     anywhere = pl.BlockSpec(memory_space=pl.ANY)
     dma = pltpu.SemaphoreType.DMA
     result = pl.pallas_call(
         functools.partial(kernel, panels, members, per_sweep, step, chunks, width),
         out_shape=jax.ShapeDtypeStruct((units, step, cols), jnp.float32),
-        in_specs=[smem, smem, anywhere, vmem, vmem],
+        in_specs=[anywhere] * 5,
         out_specs=anywhere,
         scratch_shapes=[
+            pltpu.SMEM(offsets.shape, jnp.int32),
+            pltpu.SMEM(owners.shape, jnp.int32),
+            pltpu.VMEM(reflectors.shape, jnp.float32),
+            pltpu.VMEM(inner_factors.shape, jnp.float32),
+            pltpu.VMEM((chunks, step, width), jnp.float32),
             pltpu.VMEM((chunks, units, step, width), jnp.float32),
             pltpu.VMEM((chunks, step, width), jnp.float32),
             pltpu.VMEM((4, step, width), jnp.float32),
@@ -255,6 +360,9 @@
             pltpu.VMEM((blocks, step, 2 * step), jnp.bfloat16),
             pltpu.VMEM((blocks, 2 * step, step), jnp.bfloat16),
             pltpu.VMEM((blocks, 2 * step, step), jnp.bfloat16),
+            dma((4,)),
+            dma((chunks,)),
+            dma((chunks,)),
             dma((chunks,)),
             dma((chunks,)),
             dma((chunks,)),
@@ -273,7 +381,7 @@
             bytes_accessed=2 * 4 * rows_dev * cols,
             transcendentals=0,
         ),
-    )(places, owners, vectors.reshape(units, step, cols), reflectors, inner_factors)
+    )(offsets, owners, vectors.reshape(units, step, cols), reflectors, inner_factors)
     return result.reshape(rows_dev, cols)
 
 

time: 100 us -> 126 us (1.26)
  the two profiles are of different devices: /device:TPU:16 before, /device:TPU:8 now
where the time goes in v2:
time: 126 us; the launch traced here: 125 us
  Pallas kernels  116 us (92%)
  local copies, waits for them, and re-layouts  9.28 us (7%)
    pallas_call x1, Pallas kernels, shards(): pl.pallas_call(functools.partial(kernel, panels, members, per_sweep, step...  116 us
    unnamed x9, local copies, waits for them, and re-layouts  9.28 us

profile of v2, /device:TPU:8, one launch (start us, length us, event | category | flops | bytes accessed | tf_op | source)
XLA Modules:
  0.0 125.3 jit_solution(487203758194010671)
XLA Ops:
  0.0 0.0 copy-start
  0.0 1.0 copy-done
  1.0 0.0 copy-start.1
  1.0 0.9 copy-done.1
  2.0 0.0 copy-start.2
  2.0 0.7 copy-done.2
  2.7 0.0 copy-start.3
  2.7 0.7 copy-done.3
  3.4 116.0 %shard_map.55 = f32[4,256,1536]{2,1,0:T(8,128)} custom-call(s32[2,2]{1,0:T(2,128)S(1)} %copy-done.2, s32[2,2]{1,0:T(2,128)S(1)} %copy-done.3, f32[4,256,1536]{2,1,0:T(8,128)} %bitcast.3, f32[4,128,256]{2,1,0:T(8,128)S(1)} %copy-done, f32[4,64,256]{2,1,0:T(8,128)S(1)} %copy-done.1), custom_call_target="tpu_custom_call" | custom-call | flops 9663676416 | bytes 12582912 | tf_op jit(solution)/shard_map/pallas_call | solution.py:344
  119.3 5.9 %copy.7 = f32[1024,1536]{1,0:T(8,128)} copy(f32[1024,1536]{1,0:T(8,128)} %bitcast.2) | data formatting | bytes 12582912
Async XLA Ops:
  0.0 1.0 copy-start
  1.0 0.9 copy-start.1
  2.0 0.7 copy-start.2
  2.7 0.7 copy-start.3

commit v3 on v2

--- a/solution.py
+++ b/solution.py
@@ -261,28 +261,31 @@
 
     each(lambda chunk: load(chunk).wait())
 
-    for block, (sweep, index) in enumerate(stored[:-1]):
+    def run(block, chunk):
+        change(block, current[chunk, first_unit(block)], current[chunk, lower_unit(block)])
+        apply_change(block, chunk, sum(stored[block]))
+
+    def begin(chunk):
+        run(0, chunk)
+
+        @pl.when(jnp.logical_not(is_first))
+        def _():
+            start_back(chunk)
+
+        @pl.when(is_first)
+        def _():
+            store_head(chunk).start()
+
+    last = len(stored) - 1
+    fetch(0)
+    each(begin)
+    for block in range(1, len(stored)):
         fetch(block)
 
-        def run(chunk, block=block, lowest=sweep + index):
-            change(block, current[chunk, first_unit(block)], current[chunk, lower_unit(block)])
-            apply_change(block, chunk, lowest)
-            if block == 0:
-
-                @pl.when(jnp.logical_not(is_first))
-                def _():
-                    start_back(chunk)
-
-                @pl.when(is_first)
-                def _():
-                    store_head(chunk).start()
-
-        each(run)
-
-    last = len(stored) - 1
-    fetch(last)
-
     def finish(chunk):
+        for block in range(1, last):
+            run(block, chunk)
+
         @pl.when(is_last)
         def _():
             below[chunk] = current[chunk, lower_unit(last)]
@@ -336,7 +339,7 @@
     blocks, basis_rows, step = reflectors.shape
     inner_rows = inner_factors.shape[1]
     per_sweep = offsets.shape[1]
-    width = 128
+    width = 256 if cols % 256 == 0 else 128
     chunks = cols // width
     units = rows_dev // step
     anywhere = pl.BlockSpec(memory_space=pl.ANY)
@@ -374,7 +377,7 @@
             dma((chunks,)),
         ],
         compiler_params=pltpu.CompilerParams(
-            collective_id=0, has_side_effects=True, vmem_limit_bytes=48 * 1024 * 1024
+            collective_id=0, has_side_effects=True, vmem_limit_bytes=60 * 1024 * 1024
         ),
         cost_estimate=pl.CostEstimate(
             flops=2 * 3 * 4 * blocks * step * step * cols,

time: 126 us -> 103 us (0.82)
  the two profiles are of different devices: /device:TPU:8 before, /device:TPU:16 now
where the time goes in v3:
time: 103 us
  Pallas kernels  97.2 us (94%)
  local copies, waits for them, and re-layouts  5.93 us (6%)
    pallas_call x1, Pallas kernels, shards(): pl.pallas_call(functools.partial(kernel, panels, members, per_sweep, step...  97.2 us
    unnamed x1, local copies, waits for them, and re-layouts  5.93 us

profile of v3, /device:TPU:16, one launch (start us, length us, event | category | flops | bytes accessed | tf_op | source)
XLA Modules:
  0.0 103.1 jit_solution(14751343893205419805)
XLA Ops:
  0.0 97.2 %shard_map.55 = f32[4,256,1536]{2,1,0:T(8,128)} custom-call(s32[2,2]{1,0:T(2,128)} %offsets_in.1, s32[2,2]{1,0:T(2,128)} %owners_in.1, f32[4,256,1536]{2,1,0:T(8,128)} %bitcast.3, f32[4,128,256]{2,1,0:T(8,128)} %reflectors_in.1, f32[4,64,256]{2,1,0:T(8,128)} %inner_in.1), custom_call_target="tpu_custom_call" | custom-call | flops 9663676416 | bytes 12582912 | tf_op jit(solution)/shard_map/pallas_call | solution.py:347
  97.2 5.9 %copy.7 = f32[1024,1536]{1,0:T(8,128)} copy(f32[1024,1536]{1,0:T(8,128)} %bitcast.2) | data formatting | bytes 12582912

commit v4 on v3

--- a/solution.py
+++ b/solution.py
@@ -27,9 +27,9 @@
 
 def kernel(
     panels, members, per_sweep, step, chunks, width,
-    offsets_in, owners_in, vectors, reflectors_in, inner_in, out,
-    offsets, owners, reflectors, inner, relay, current, below, update, gathered, basis_high, basis_low, mixed_high, mixed_low,
-    early_sem, relay_send, relay_recv, load_sem, store_sem, head_sem, part_send, part_recv, back_send, back_recv, fore_send, fore_recv,
+    offsets_in, owners_in, vectors, reflectors_in, inner_in, first_out, rest_out,
+    offsets, owners, reflectors, inner, current, below, update, gathered, basis_high, basis_low, mixed_high, mixed_low,
+    early_sem, load_sem, store_sem, head_sem, part_send, part_recv, back_send, back_recv, fore_send, fore_recv,
 ):
     panel = lax.axis_index("row")
     me = lax.axis_index("vec")
@@ -40,9 +40,6 @@
     units = vectors.shape[0]
     basis_rows = reflectors.shape[1]
     first_row = panel * units * step
-    pairs = panels // 2
-    is_odd = panel % 2 == 1
-    pair = panel // 2
     is_first = panel == 0
     is_last = panel == panels - 1
     stored = [(sweep, index) for sweep in range(2) for index in range(per_sweep)]
@@ -56,23 +53,14 @@
     def store(chunk):
         return pltpu.make_async_copy(
             current.at[chunk, pl.ds(1, units - 1)],
-            out.at[pl.ds(1, units - 1), :, columns(chunk)],
+            rest_out.at[:, :, columns(chunk)],
             store_sem.at[chunk],
         )
 
     def store_head(chunk):
         return pltpu.make_async_copy(
-            current.at[chunk, 0], out.at[0, :, columns(chunk)], head_sem.at[chunk]
-        )
-
-    def turn(chunk, share):
-        return ((chunk + 1) * share) // pairs - (chunk * share) // pairs == 1
-
-    def back_turn(chunk, source_pair):
-        return turn(chunk, pairs - source_pair)
-
-    def fore_turn(chunk, source_pair):
-        return turn(chunk, source_pair + 1)
+            current.at[chunk, 0], head(chunk), head_sem.at[chunk]
+        )
 
     def remote(source, target, send_sem, recv_sem, row):
         return pltpu.make_async_remote_copy(
@@ -85,74 +73,13 @@
         )
 
     def head(chunk):
-        return out.at[0, :, columns(chunk)]
+        return first_out.at[:, columns(chunk)]
 
     def send_back(chunk):
         return remote(current.at[chunk, 0], below.at[chunk], back_send.at[chunk], back_recv.at[chunk], panel - 1)
 
-    def send_back_far(chunk):
-        return remote(current.at[chunk, 0], relay.at[chunk], back_send.at[chunk], relay_recv.at[chunk], panel - 2)
-
     def send_fore(chunk):
         return remote(below.at[chunk], head(chunk), fore_send.at[chunk], fore_recv.at[chunk], panel + 1)
-
-    def send_fore_far(chunk):
-        return remote(below.at[chunk], relay.at[chunk], fore_send.at[chunk], relay_recv.at[chunk], panel + 2)
-
-    def pass_back(chunk):
-        return remote(relay.at[chunk], below.at[chunk], relay_send.at[chunk], back_recv.at[chunk], panel + 1)
-
-    def pass_fore(chunk):
-        return remote(relay.at[chunk], head(chunk), relay_send.at[chunk], fore_recv.at[chunk], panel - 1)
-
-    passes_back = jnp.logical_and(jnp.logical_not(is_odd), panel + 2 < panels)
-    passes_fore = jnp.logical_and(is_odd, panel > 1)
-
-    def both(left, right):
-        return jnp.logical_and(left, right)
-
-    def start_back(chunk):
-        far = both(jnp.logical_not(is_odd), back_turn(chunk, pair))
-
-        @pl.when(far)
-        def _():
-            send_back_far(chunk).start()
-
-        @pl.when(jnp.logical_not(far))
-        def _():
-            send_back(chunk).start()
-
-    def start_fore(chunk):
-        far = both(both(is_odd, panel + 2 < panels), fore_turn(chunk, pair))
-
-        @pl.when(far)
-        def _():
-            send_fore_far(chunk).start()
-
-        @pl.when(jnp.logical_not(far))
-        def _():
-            send_fore(chunk).start()
-
-    def hand_back(chunk):
-        @pl.when(both(passes_back, both(chunk < chunks, back_turn(chunk, pair + 1))))
-        def _():
-            send_back_far(chunk).wait_recv()
-            pass_back(chunk).start()
-
-    def hand_fore(chunk):
-        @pl.when(both(passes_fore, both(chunk >= 0, fore_turn(chunk, pair - 1))))
-        def _():
-            send_fore_far(chunk).wait_recv()
-            pass_fore(chunk).start()
-
-    def settle(chunk):
-        handed = jnp.logical_or(
-            both(passes_back, back_turn(chunk, pair + 1)), both(passes_fore, fore_turn(chunk, pair - 1))
-        )
-
-        @pl.when(handed)
-        def _():
-            pass_back(chunk).wait_send()
 
     def send_part(block, part, slot, target):
         return pltpu.make_async_remote_copy(
@@ -197,14 +124,6 @@
     def _():
         greet(panel + 1, me)
 
-    @pl.when(panel > 1)
-    def _():
-        greet(panel - 2, me)
-
-    @pl.when(panel + 2 < panels)
-    def _():
-        greet(panel + 2, me)
-
     for copy in early:
         copy.wait()
 
@@ -217,8 +136,7 @@
     update[3] = jnp.zeros_like(update[3])
 
     beside = jnp.minimum(panel, 1) + jnp.minimum(panels - 1 - panel, 1)
-    beyond = jnp.minimum(panel // 2, 1) + jnp.minimum((panels - 1 - panel) // 2, 1)
-    pl.semaphore_wait(barrier, chips + beside + beyond)
+    pl.semaphore_wait(barrier, chips + beside)
 
     for block in range(len(stored)):
         for distance in range(1, chips):
@@ -270,7 +188,7 @@
 
         @pl.when(jnp.logical_not(is_first))
         def _():
-            start_back(chunk)
+            send_back(chunk).start()
 
         @pl.when(is_first)
         def _():
@@ -299,17 +217,12 @@
         @pl.when(jnp.logical_not(is_last))
         def _():
             below[chunk] = below[chunk] - update[2]
-            start_fore(chunk)
-
-        hand_back(chunk + 1)
-        hand_fore(chunk - 1)
+            send_fore(chunk).start()
+
         apply_change(last, chunk, per_sweep)
         store(chunk).start()
 
-    hand_back(0)
     each(finish)
-    hand_fore(chunks - 1)
-    each(settle)
 
     for block in range(len(stored)):
         for slot in range(members - 1):
@@ -344,17 +257,19 @@
     units = rows_dev // step
     anywhere = pl.BlockSpec(memory_space=pl.ANY)
     dma = pltpu.SemaphoreType.DMA
-    result = pl.pallas_call(
+    first, rest = pl.pallas_call(
         functools.partial(kernel, panels, members, per_sweep, step, chunks, width),
-        out_shape=jax.ShapeDtypeStruct((units, step, cols), jnp.float32),
+        out_shape=[
+            jax.ShapeDtypeStruct((step, cols), jnp.float32),
+            jax.ShapeDtypeStruct((units - 1, step, cols), jnp.float32),
+        ],
         in_specs=[anywhere] * 5,
-        out_specs=anywhere,
+        out_specs=[anywhere] * 2,
         scratch_shapes=[
             pltpu.SMEM(offsets.shape, jnp.int32),
             pltpu.SMEM(owners.shape, jnp.int32),
             pltpu.VMEM(reflectors.shape, jnp.float32),
             pltpu.VMEM(inner_factors.shape, jnp.float32),
-            pltpu.VMEM((chunks, step, width), jnp.float32),
             pltpu.VMEM((chunks, units, step, width), jnp.float32),
             pltpu.VMEM((chunks, step, width), jnp.float32),
             pltpu.VMEM((4, step, width), jnp.float32),
@@ -364,8 +279,6 @@
             pltpu.VMEM((blocks, 2 * step, step), jnp.bfloat16),
             pltpu.VMEM((blocks, 2 * step, step), jnp.bfloat16),
             dma((4,)),
-            dma((chunks,)),
-            dma((chunks,)),
             dma((chunks,)),
             dma((chunks,)),
             dma((chunks,)),
@@ -385,7 +298,7 @@
             transcendentals=0,
         ),
     )(offsets, owners, vectors.reshape(units, step, cols), reflectors, inner_factors)
-    return result.reshape(rows_dev, cols)
+    return jnp.concatenate([first, rest.reshape(rows_dev - step, cols)], 0)
 
 
 def solution(mesh):

time: 103 us -> 96 us (0.932); the launches traced: 103 us -> 94.6 us
  Pallas kernels: 97.2 us -> 88.6 us
  other arithmetic: 0 us -> 5.99 us
  local copies, waits for them, and re-layouts: 5.93 us -> 0 us
    pallas_call x1, Pallas kernels: 97.2 us -> 88.6 us  [shards(): pl.pallas_call(functools.partial(kernel, panels, members, per_sweep, step...]
    concatenate x0 -> x1, other arithmetic: none -> 5.99 us  [shards(): return jnp.concatenate([first, rest.reshape(rows_dev - step, cols)], 0)]
    unnamed x1 -> x0, local copies, waits for them, and re-layouts: 5.93 us -> none
where the time goes in v4:
time: 96 us; the launch traced here: 94.6 us
  Pallas kernels  88.6 us (92%)
  other arithmetic  5.99 us (6%)
    pallas_call x1, Pallas kernels, shards(): pl.pallas_call(functools.partial(kernel, panels, members, per_sweep, step...  88.6 us
    concatenate x1, other arithmetic, shards(): return jnp.concatenate([first, rest.reshape(rows_dev - step, cols)], 0)  5.99 us

profile of v4, /device:TPU:16, one launch (start us, length us, event | category | flops | bytes accessed | tf_op | source)
XLA Modules:
  0.0 94.6 jit_solution(458073047475313719)
XLA Ops:
  0.0 88.6 %shard_map.55 = (f32[256,1536]{1,0:T(8,128)}, f32[3,256,1536]{2,1,0:T(8,128)}) custom-call(s32[2,2]{1,0:T(2,128)} %offsets_in.1, s32[2,2]{1,0:T(2,128)} %owners_in.1, f32[4,256,1536]{2,1,0:T(8,128)} %bitcast.3, f32[4,128,256]{2,1,0:T(8,128)} %reflectors_in.1, f32[4,64,256]{2,1,0:T(8,128)} %inner_in.1), custom_call_target="tpu_custom_call" | custom-call | flops 9663676416 | bytes 12582912 | tf_op jit(solution)/shard_map/pallas_call | solution.py:260
  88.6 6.0 %pad_maximum_fusion = f32[1024,1536]{1,0:T(8,128)} fusion(f32[768,1536]{1,0:T(8,128)} %bitcast.2, f32[256,1536]{1,0:T(8,128)} %get-tuple-element.7), kind=kLoop, calls=%fused_computation | loop fusion | flops 1572864 | bytes 12582912 | tf_op jit(solution)/shard_map/concatenate | solution.py:301

commit v5 on v4

--- a/solution.py
+++ b/solution.py
@@ -28,8 +28,8 @@
 def kernel(
     panels, members, per_sweep, step, chunks, width,
     offsets_in, owners_in, vectors, reflectors_in, inner_in, first_out, rest_out,
-    offsets, owners, reflectors, inner, current, below, update, gathered, basis_high, basis_low, mixed_high, mixed_low,
-    early_sem, load_sem, store_sem, head_sem, part_send, part_recv, back_send, back_recv, fore_send, fore_recv,
+    offsets, owners, reflectors, inner, relay, current, below, update, gathered, basis_high, basis_low, mixed_high, mixed_low,
+    early_sem, relay_send, relay_recv, load_sem, store_sem, head_sem, part_send, part_recv, back_send, back_recv, fore_send, fore_recv,
 ):
     panel = lax.axis_index("row")
     me = lax.axis_index("vec")
@@ -59,8 +59,23 @@
 
     def store_head(chunk):
         return pltpu.make_async_copy(
-            current.at[chunk, 0], head(chunk), head_sem.at[chunk]
+            current.at[chunk, 0], first_out.at[:, columns(chunk)], head_sem.at[chunk]
         )
+
+    half = step // 2
+    pieces = 2 * chunks
+    pairs = panels // 2
+    is_odd = panel % 2 == 1
+    pair = panel // 2
+
+    def both(left, right):
+        return jnp.logical_and(left, right)
+
+    def back_turn(piece, source_pair):
+        return piece < (pieces * (pairs - source_pair)) // pairs
+
+    def fore_turn(piece, source_pair):
+        return piece < (pieces * (source_pair + 1)) // pairs
 
     def remote(source, target, send_sem, recv_sem, row):
         return pltpu.make_async_remote_copy(
@@ -72,14 +87,93 @@
             device_id_type=MESH,
         )
 
-    def head(chunk):
-        return first_out.at[:, columns(chunk)]
-
-    def send_back(chunk):
-        return remote(current.at[chunk, 0], below.at[chunk], back_send.at[chunk], back_recv.at[chunk], panel - 1)
-
-    def send_fore(chunk):
-        return remote(below.at[chunk], head(chunk), fore_send.at[chunk], fore_recv.at[chunk], panel + 1)
+    def top(chunk, side):
+        return current.at[chunk, 0, pl.ds(side * half, half)]
+
+    def low(chunk, side):
+        return below.at[chunk, pl.ds(side * half, half)]
+
+    def head(chunk, side):
+        return first_out.at[pl.ds(side * half, half), columns(chunk)]
+
+    def send_back(chunk, side):
+        at = 2 * chunk + side
+        return remote(top(chunk, side), low(chunk, side), back_send.at[at], back_recv.at[at], panel - 1)
+
+    def send_back_far(chunk, side):
+        at = 2 * chunk + side
+        return remote(top(chunk, side), relay.at[at], back_send.at[at], relay_recv.at[at], panel - 2)
+
+    def send_fore(chunk, side):
+        at = 2 * chunk + side
+        return remote(low(chunk, side), head(chunk, side), fore_send.at[at], fore_recv.at[at], panel + 1)
+
+    def send_fore_far(chunk, side):
+        at = 2 * chunk + side
+        return remote(low(chunk, side), relay.at[at], fore_send.at[at], relay_recv.at[at], panel + 2)
+
+    def pass_back(chunk, side):
+        at = 2 * chunk + side
+        return remote(relay.at[at], low(chunk, side), relay_send.at[at], back_recv.at[at], panel + 1)
+
+    def pass_fore(chunk, side):
+        at = 2 * chunk + side
+        return remote(relay.at[at], head(chunk, side), relay_send.at[at], fore_recv.at[at], panel - 1)
+
+    passes_back = both(jnp.logical_not(is_odd), panel + 2 < panels)
+    passes_fore = both(is_odd, panel > 1)
+
+    def choose(far, far_copy, near_copy):
+        @pl.when(far)
+        def _():
+            far_copy.start()
+
+        @pl.when(jnp.logical_not(far))
+        def _():
+            near_copy.start()
+
+    def start_back(chunk):
+        for side in range(2):
+            far = both(jnp.logical_not(is_odd), back_turn(2 * chunk + side, pair))
+            choose(far, send_back_far(chunk, side), send_back(chunk, side))
+
+    def start_fore(chunk):
+        for side in range(2):
+            far = both(both(is_odd, panel + 2 < panels), fore_turn(2 * chunk + side, pair))
+            choose(far, send_fore_far(chunk, side), send_fore(chunk, side))
+
+    def hands_back(chunk, side):
+        return both(passes_back, both(chunk < chunks, back_turn(2 * chunk + side, pair + 1)))
+
+    def hands_fore(chunk, side):
+        return both(passes_fore, both(chunk >= 0, fore_turn(2 * chunk + side, pair - 1)))
+
+    def hand_back(chunk):
+        for side in range(2):
+
+            @pl.when(hands_back(chunk, side))
+            def _(side=side):
+                send_back_far(chunk, side).wait_recv()
+                pass_back(chunk, side).start()
+
+    def hand_fore(chunk):
+        for side in range(2):
+
+            @pl.when(hands_fore(chunk, side))
+            def _(side=side):
+                send_fore_far(chunk, side).wait_recv()
+                pass_fore(chunk, side).start()
+
+    def settle(chunk):
+        for side in range(2):
+
+            @pl.when(jnp.logical_or(hands_back(chunk, side), hands_fore(chunk, side)))
+            def _(side=side):
+                pass_back(chunk, side).wait_send()
+
+    def sides(body):
+        for side in range(2):
+            body(side)
 
     def send_part(block, part, slot, target):
         return pltpu.make_async_remote_copy(
@@ -124,6 +218,14 @@
     def _():
         greet(panel + 1, me)
 
+    @pl.when(panel > 1)
+    def _():
+        greet(panel - 2, me)
+
+    @pl.when(panel + 2 < panels)
+    def _():
+        greet(panel + 2, me)
+
     for copy in early:
         copy.wait()
 
@@ -136,7 +238,8 @@
     update[3] = jnp.zeros_like(update[3])
 
     beside = jnp.minimum(panel, 1) + jnp.minimum(panels - 1 - panel, 1)
-    pl.semaphore_wait(barrier, chips + beside)
+    beyond = jnp.minimum(panel // 2, 1) + jnp.minimum((panels - 1 - panel) // 2, 1)
+    pl.semaphore_wait(barrier, chips + beside + beyond)
 
     for block in range(len(stored)):
         for distance in range(1, chips):
@@ -188,7 +291,7 @@
 
         @pl.when(jnp.logical_not(is_first))
         def _():
-            send_back(chunk).start()
+            start_back(chunk)
 
         @pl.when(is_first)
         def _():
@@ -204,25 +307,31 @@
         for block in range(1, last):
             run(block, chunk)
 
+        hand_back(chunk + 1)
+
         @pl.when(is_last)
         def _():
             below[chunk] = current[chunk, lower_unit(last)]
 
         @pl.when(jnp.logical_not(is_last))
         def _():
-            send_back(chunk).wait_recv()
+            sides(lambda side: send_back(chunk, side).wait_recv())
 
         change(last, current[chunk, first_unit(last)], below[chunk])
 
         @pl.when(jnp.logical_not(is_last))
         def _():
             below[chunk] = below[chunk] - update[2]
-            send_fore(chunk).start()
-
+            start_fore(chunk)
+
+        hand_fore(chunk - 1)
         apply_change(last, chunk, per_sweep)
         store(chunk).start()
 
+    hand_back(0)
     each(finish)
+    hand_fore(chunks - 1)
+    each(settle)
 
     for block in range(len(stored)):
         for slot in range(members - 1):
@@ -234,17 +343,17 @@
 
     @pl.when(jnp.logical_not(is_first))
     def _():
-        each(lambda chunk: send_back(chunk).wait_send())
+        each(lambda chunk: sides(lambda side: send_back(chunk, side).wait_send()))
 
     each(lambda chunk: store(chunk).wait())
 
     @pl.when(jnp.logical_not(is_last))
     def _():
-        each(lambda chunk: send_fore(chunk).wait_send())
+        each(lambda chunk: sides(lambda side: send_fore(chunk, side).wait_send()))
 
     @pl.when(jnp.logical_not(is_first))
     def _():
-        each(lambda chunk: send_fore(chunk).wait_recv())
+        each(lambda chunk: sides(lambda side: send_fore(chunk, side).wait_recv()))
 
 
 def shards(panels, members, vectors, reflectors, inner_factors, offsets, owners):
@@ -270,6 +379,7 @@
             pltpu.SMEM(owners.shape, jnp.int32),
             pltpu.VMEM(reflectors.shape, jnp.float32),
             pltpu.VMEM(inner_factors.shape, jnp.float32),
+            pltpu.VMEM((2 * chunks, step // 2, width), jnp.float32),
             pltpu.VMEM((chunks, units, step, width), jnp.float32),
             pltpu.VMEM((chunks, step, width), jnp.float32),
             pltpu.VMEM((4, step, width), jnp.float32),
@@ -279,15 +389,17 @@
             pltpu.VMEM((blocks, 2 * step, step), jnp.bfloat16),
             pltpu.VMEM((blocks, 2 * step, step), jnp.bfloat16),
             dma((4,)),
+            dma((2 * chunks,)),
+            dma((2 * chunks,)),
             dma((chunks,)),
             dma((chunks,)),
             dma((chunks,)),
             dma((blocks, members - 1)),
             dma((blocks, members)),
-            dma((chunks,)),
-            dma((chunks,)),
-            dma((chunks,)),
-            dma((chunks,)),
+            dma((2 * chunks,)),
+            dma((2 * chunks,)),
+            dma((2 * chunks,)),
+            dma((2 * chunks,)),
         ],
         compiler_params=pltpu.CompilerParams(
             collective_id=0, has_side_effects=True, vmem_limit_bytes=60 * 1024 * 1024

time: 96 us -> 102 us (1.062)
  Pallas kernels: 88.6 us -> 94.8 us
    pallas_call x1, Pallas kernels: 88.6 us -> 94.8 us  [shards(): pl.pallas_call(functools.partial(kernel, panels, members, per_sweep, step...]
where the time goes in v5:
time: 102 us; the launch traced here: 101 us
  Pallas kernels  94.8 us (93%)
  other arithmetic  5.99 us (6%)
    pallas_call x1, Pallas kernels, shards(): pl.pallas_call(functools.partial(kernel, panels, members, per_sweep, step...  94.8 us
    concatenate x1, other arithmetic, shards(): return jnp.concatenate([first, rest.reshape(rows_dev - step, cols)], 0)  5.99 us

profile of v5, /device:TPU:16, one launch (start us, length us, event | category | flops | bytes accessed | tf_op | source)
XLA Modules:
  0.0 100.8 jit_solution(10927326533530321276)
XLA Ops:
  0.0 94.8 %shard_map.55 = (f32[256,1536]{1,0:T(8,128)}, f32[3,256,1536]{2,1,0:T(8,128)}) custom-call(s32[2,2]{1,0:T(2,128)} %offsets_in.1, s32[2,2]{1,0:T(2,128)} %owners_in.1, f32[4,256,1536]{2,1,0:T(8,128)} %bitcast.3, f32[4,128,256]{2,1,0:T(8,128)} %reflectors_in.1, f32[4,64,256]{2,1,0:T(8,128)} %inner_in.1), custom_call_target="tpu_custom_call" | custom-call | flops 9663676416 | bytes 12582912 | tf_op jit(solution)/shard_map/pallas_call | solution.py:369
  94.8 6.0 %pad_maximum_fusion = f32[1024,1536]{1,0:T(8,128)} fusion(f32[768,1536]{1,0:T(8,128)} %bitcast.2, f32[256,1536]{1,0:T(8,128)} %get-tuple-element.7), kind=kLoop, calls=%fused_computation | loop fusion | flops 1572864 | bytes 12582912 | tf_op jit(solution)/shard_map/concatenate | solution.py:413

commit v6 on v4

--- a/solution.py
+++ b/solution.py
@@ -138,10 +138,12 @@
     beside = jnp.minimum(panel, 1) + jnp.minimum(panels - 1 - panel, 1)
     pl.semaphore_wait(barrier, chips + beside)
 
-    for block in range(len(stored)):
+    def spread(block):
         for distance in range(1, chips):
             send_part(block, me, distance, other_chip(distance) * 2 + core).start()
         send_part(block, me, 0, sibling).start()
+
+    spread(0)
 
     def fetch(block):
         for distance in range(1, chips):
@@ -152,6 +154,9 @@
         for distance in range(1, chips):
             part = other_chip(distance) * 2 + 1 - core
             send_part(block, part, chips - 1 + distance, sibling).wait_recv()
+        if block == 0:
+            for later in range(1, len(stored)):
+                spread(later)
         basis = gathered[block, :, :basis_rows, :].reshape(2 * step, step)
         coupling = gathered[block, :, basis_rows:, :].reshape(step, step)
         high, low = split(basis)

time: 96 us -> 95.3 us (level)
  Pallas kernels: 88.6 us -> 87.5 us
    pallas_call x1, Pallas kernels: 88.6 us -> 87.5 us  [shards(): pl.pallas_call(functools.partial(kernel, panels, members, per_sweep, step...]
where the time goes in v6:
time: 95.3 us; the launch traced here: 93.5 us
  Pallas kernels  87.5 us (92%)
  other arithmetic  5.99 us (6%)
    pallas_call x1, Pallas kernels, shards(): pl.pallas_call(functools.partial(kernel, panels, members, per_sweep, step...  87.5 us
    concatenate x1, other arithmetic, shards(): return jnp.concatenate([first, rest.reshape(rows_dev - step, cols)], 0)  5.99 us

profile of v6, /device:TPU:16, one launch (start us, length us, event | category | flops | bytes accessed | tf_op | source)
XLA Modules:
  0.0 93.5 jit_solution(9007869091773487805)
XLA Ops:
  0.0 87.5 %shard_map.55 = (f32[256,1536]{1,0:T(8,128)}, f32[3,256,1536]{2,1,0:T(8,128)}) custom-call(s32[2,2]{1,0:T(2,128)} %offsets_in.1, s32[2,2]{1,0:T(2,128)} %owners_in.1, f32[4,256,1536]{2,1,0:T(8,128)} %bitcast.3, f32[4,128,256]{2,1,0:T(8,128)} %reflectors_in.1, f32[4,64,256]{2,1,0:T(8,128)} %inner_in.1), custom_call_target="tpu_custom_call" | custom-call | flops 9663676416 | bytes 12582912 | tf_op jit(solution)/shard_map/pallas_call | solution.py:265
  87.5 6.0 %pad_maximum_fusion = f32[1024,1536]{1,0:T(8,128)} fusion(f32[768,1536]{1,0:T(8,128)} %bitcast.2, f32[256,1536]{1,0:T(8,128)} %get-tuple-element.7), kind=kLoop, calls=%fused_computation | loop fusion | flops 1572864 | bytes 12582912 | tf_op jit(solution)/shard_map/concatenate | solution.py:306

commit v7 on v5

--- a/solution.py
+++ b/solution.py
@@ -241,10 +241,12 @@
     beyond = jnp.minimum(panel // 2, 1) + jnp.minimum((panels - 1 - panel) // 2, 1)
     pl.semaphore_wait(barrier, chips + beside + beyond)
 
-    for block in range(len(stored)):
+    def spread(block):
         for distance in range(1, chips):
             send_part(block, me, distance, other_chip(distance) * 2 + core).start()
         send_part(block, me, 0, sibling).start()
+
+    spread(0)
 
     def fetch(block):
         for distance in range(1, chips):
@@ -255,6 +257,9 @@
         for distance in range(1, chips):
             part = other_chip(distance) * 2 + 1 - core
             send_part(block, part, chips - 1 + distance, sibling).wait_recv()
+        if block == 0:
+            for later in range(1, len(stored)):
+                spread(later)
         basis = gathered[block, :, :basis_rows, :].reshape(2 * step, step)
         coupling = gathered[block, :, basis_rows:, :].reshape(step, step)
         high, low = split(basis)
@@ -289,7 +294,7 @@
     def begin(chunk):
         run(0, chunk)
 
-        @pl.when(jnp.logical_not(is_first))
+        @pl.when(both(jnp.logical_not(is_first), chunk < ahead))
         def _():
             start_back(chunk)
 
@@ -298,12 +303,21 @@
             store_head(chunk).start()
 
     last = len(stored) - 1
+    ahead = 3
     fetch(0)
     each(begin)
     for block in range(1, len(stored)):
         fetch(block)
 
     def finish(chunk):
+        @pl.when(jnp.logical_not(is_first))
+        def _():
+            sides(lambda side: send_back(chunk, side).wait_send())
+
+        @pl.when(both(jnp.logical_not(is_first), chunk + ahead < chunks))
+        def _():
+            start_back(chunk + ahead)
+
         for block in range(1, last):
             run(block, chunk)
 
@@ -340,10 +354,6 @@
     @pl.when(is_first)
     def _():
         each(lambda chunk: store_head(chunk).wait())
-
-    @pl.when(jnp.logical_not(is_first))
-    def _():
-        each(lambda chunk: sides(lambda side: send_back(chunk, side).wait_send()))
 
     each(lambda chunk: store(chunk).wait())
 

time: 102 us -> 108 us (1.059)
  Pallas kernels: 94.8 us -> 101 us
    pallas_call x1, Pallas kernels: 94.8 us -> 101 us  [shards(): pl.pallas_call(functools.partial(kernel, panels, members, per_sweep, step...]
where the time goes in v7:
time: 108 us; the launch traced here: 107 us
  Pallas kernels  101 us (94%)
  other arithmetic  5.99 us (6%)
    pallas_call x1, Pallas kernels, shards(): pl.pallas_call(functools.partial(kernel, panels, members, per_sweep, step...  101 us
    concatenate x1, other arithmetic, shards(): return jnp.concatenate([first, rest.reshape(rows_dev - step, cols)], 0)  5.99 us

profile of v7, /device:TPU:16, one launch (start us, length us, event | category | flops | bytes accessed | tf_op | source)
XLA Modules:
  0.0 107.4 jit_solution(9992712295849599822)
XLA Ops:
  0.0 101.4 %shard_map.55 = (f32[256,1536]{1,0:T(8,128)}, f32[3,256,1536]{2,1,0:T(8,128)}) custom-call(s32[2,2]{1,0:T(2,128)} %offsets_in.1, s32[2,2]{1,0:T(2,128)} %owners_in.1, f32[4,256,1536]{2,1,0:T(8,128)} %bitcast.3, f32[4,128,256]{2,1,0:T(8,128)} %reflectors_in.1, f32[4,64,256]{2,1,0:T(8,128)} %inner_in.1), custom_call_target="tpu_custom_call" | custom-call | flops 9663676416 | bytes 12582912 | tf_op jit(solution)/shard_map/pallas_call | solution.py:379
  101.4 6.0 %pad_maximum_fusion = f32[1024,1536]{1,0:T(8,128)} fusion(f32[768,1536]{1,0:T(8,128)} %bitcast.2, f32[256,1536]{1,0:T(8,128)} %get-tuple-element.7), kind=kLoop, calls=%fused_computation | loop fusion | flops 1572864 | bytes 12582912 | tf_op jit(solution)/shard_map/concatenate | solution.py:423
